TPU v7x, 32 devices: a whole 2x2x4 slice. The times are simulated.
32 devices in a mesh: gx: 2 (over x), gy: 4 (over z), gz: 4 (over y, core).
Axes of the slice: x: 2, y: 2, z: 4, core: 2. Of those that a mesh axis runs over, the one named last changes fastest.
Arguments:
- fields: float32 [5, 64, 256, 512], P(None, 'gx', 'gy', 'gz'), may hold values from -4 to 9
- viscous: float32 [5], replicated, may hold values from 1 to 8000
Outputs:
- updated: float32 [5, 64, 256, 512], P(None, 'gx', 'gy', 'gz')
All inputs are finite; a program needn't handle non-finite values.
Results may differ from a plain program's by a relative error of at most 0.0003.
Values sent between devices are 32-bit elements; how exact they have to be, the bound alone decides.
A program may use at most 128 MiB of HBM per device.

v0:
```python
import math

import jax
import jax.numpy as jnp
from jax import lax
from jax.sharding import PartitionSpec as P

advect = 0.3
root_ratio = (-1.0 + math.sqrt(5.0) / 3.0) * 1.5
line_gain = (1.0 + root_ratio * root_ratio) / (1.0 - root_ratio * root_ratio)
highest = lax.Precision.HIGHEST


def extended(array, sides, width):
    for axis, dim in sides:
        peers, length = (lax.axis_size(axis), array.shape[dim])
        up = [(i, (i + 1) % peers) for i in range(peers)]
        down = [(j, i) for i, j in up]
        last = lax.slice_in_dim(array, length - width, length, axis=dim)
        leading = lax.slice_in_dim(array, 0, width, axis=dim)
        before = lax.ppermute(last, axis, up)
        after = lax.ppermute(leading, axis, down)
        array = jnp.concatenate([before, array, after], axis=dim)
    return array


def carried_in(part, axis, combine, identity, reverse):
    count = lax.axis_size(axis)
    place = lax.axis_index(axis)
    ahead = count - 1 - place if reverse else place
    gathered = jax.tree.map(lambda a: lax.all_gather(a, axis), part)
    state = jax.tree.map(lambda a, e: jnp.zeros_like(a) + jnp.asarray(e, a.dtype), part, identity)

    def one(hop, state):
        source = count - 1 - hop if reverse else hop
        return combine(
            state, jax.tree.map(lambda a: lax.dynamic_index_in_dim(a, source, 0, False), gathered)
        )

    return lax.fori_loop(0, ahead, one, state)


def signed_power(exponent):
    parity = jnp.mod(exponent, 2.0)
    return (1.0 - 2.0 * parity) * jnp.exp(exponent * math.log(abs(root_ratio)))


def pade_kernel(length):
    row_index = jnp.arange(length, dtype=jnp.float32)[:, None]
    col_index = jnp.arange(length, dtype=jnp.float32)[None, :]
    offset = jnp.mod(row_index - col_index, float(length))
    closing = 1.0 - signed_power(jnp.float32(length))
    return line_gain * (signed_power(offset) + signed_power(length - offset)) / closing


def compact_source(line_block):

    def shifted(offset):
        return jnp.roll(line_block, -offset, axis=1)

    return 7.0 / 9.0 * (shifted(1) - shifted(-1)) + 1.0 / 36.0 * (shifted(2) - shifted(-2))


def span_derivative(fields):
    padded = extended(fields, (("gz", 3),), 3)
    span_count = fields.shape[3]

    def shifted(offset):
        return padded[..., 3 + offset : 3 + offset + span_count]

    return (
        45.0 * (shifted(1) - shifted(-1))
        - 9.0 * (shifted(2) - shifted(-2))
        + (shifted(3) - shifted(-3))
    ) / 60.0


def combine_wall(earlier, later_pair):
    return (later_pair[1][:, None, None] * earlier[0] + later_pair[0], earlier[1] * later_pair[1])


def wall_carries(explicit, viscous):
    row_count = explicit.shape[2]
    total_rows = row_count * lax.axis_size("gy")
    diagonal = 1.0 + 2.0 * viscous

    def pivot_step(previous, unused):
        current = 1.0 / (diagonal - viscous * viscous * previous)
        return (current, current)

    _, pivots = lax.scan(pivot_step, jnp.zeros_like(viscous), None, length=total_rows)
    pivots = lax.dynamic_slice_in_dim(pivots, lax.axis_index("gy") * row_count, row_count, 0).T
    log_gain = jnp.log(viscous[:, None] * pivots)
    inclusive = jnp.cumsum(log_gain, axis=1)
    exclusive = inclusive - log_gain
    row_index = jnp.arange(row_count)[:, None]
    col_index = jnp.arange(row_count)[None, :]
    lower_mask = col_index <= row_index
    upper_mask = col_index >= row_index
    spread = inclusive[:, :, None] - inclusive[:, None, :]
    forward_table = jnp.where(
        lower_mask, pivots[:, None, :] * jnp.exp(jnp.where(lower_mask, spread, 0.0)), 0.0
    )
    eliminated_local = jnp.einsum("fik,fxkz->fxiz", forward_table, explicit, precision=highest)
    block_gain = jnp.exp(inclusive[:, -1])
    zero_line = jnp.zeros_like(eliminated_local[:, :, -1])
    enter_low, _ = carried_in(
        (eliminated_local[:, :, -1], block_gain),
        "gy",
        combine_wall,
        (zero_line, jnp.ones_like(block_gain)),
        False,
    )
    eliminated = eliminated_local + jnp.exp(inclusive)[:, None, :, None] * enter_low[:, :, None, :]
    reach_log = exclusive[:, None, :] - exclusive[:, :, None]
    backward_table = jnp.where(upper_mask, jnp.exp(jnp.where(upper_mask, reach_log, 0.0)), 0.0)
    solved = jnp.einsum("fik,fxkz->fxiz", backward_table, eliminated, precision=highest)
    enter_high, _ = carried_in(
        (solved[:, :, 0], block_gain),
        "gy",
        combine_wall,
        (zero_line, jnp.ones_like(block_gain)),
        True,
    )
    trailing = jnp.exp(inclusive[:, -1:] - exclusive)
    return solved + trailing[:, None, :, None] * enter_high[:, :, None, :]


def shards(fields, viscous):
    span_slope = span_derivative(fields)
    line_block = lax.all_to_all(fields, "gx", split_axis=2, concat_axis=1, tiled=True)
    source = compact_source(line_block)
    kernel = pade_kernel(line_block.shape[1])
    derivative = jnp.einsum("ij,fjyz->fiyz", kernel, source, precision=highest)
    line_slope = lax.all_to_all(derivative, "gx", split_axis=1, concat_axis=2, tiled=True)
    explicit = fields - advect * fields[0] * line_slope - advect * fields[2] * span_slope
    updated = wall_carries(explicit, viscous)
    return updated


def solution(mesh):
    in_specs = (P(None, "gx", "gy", "gz"), P())
    out_specs = P(None, "gx", "gy", "gz")
    return jax.shard_map(shards, mesh=mesh, in_specs=in_specs, out_specs=out_specs, check_vma=False)
```

profile of v0, /device:TPU:0, one launch (start us, length us, event | category | flops | bytes accessed | tf_op | source)
XLA Modules:
  0.0 255.0 jit_solution(9333910514754802027)
XLA Ops:
  0.0 7.9 %copy.9 = f32[5,32,64,128]{3,1,0,2:T(8,128)} copy(f32[5,32,64,128]{3,2,1,0:T(8,128)} %param.8) | data formatting | bytes 10485760 | tf_op args[0]
  7.9 6.0 %all-to-all-start = ((f32[5,32,64,128]{3,1,0,2:T(8,128)}), f32[5,32,64,128]{3,1,0,2:T(8,128)}, u32[]{:S(2)}, u32[]{:S(2)}) async-start(f32[5,32,64,128]{3,1,0,2:T(8,128)} %copy.9), calls=%async_computation | async-start | bytes 10485760 | tf_op jit(solution)/shard_map/all_to_all | solution.py:131
  13.8 9.6 %fusion.135 = (f32[5,32,64,3]{3,2,1,0:T(8,128)}, f32[5,32,64,3]{3,2,1,0:T(8,128)}) fusion(f32[5,32,64,128]{3,2,1,0:T(8,128)} %param.8), kind=kLoop, calls=%fused_computation.145 | loop fusion | bytes 491520 | tf_op jit(solution)/shard_map/slice | solution.py:20
  23.4 3.5 %copy.23 = f32[5,32,64,3]{2,1,3,0:T(8,128)S(1)} copy(f32[5,32,64,3]{3,2,1,0:T(8,128)} %get-tuple-element.253) | data formatting | bytes 245760
  29.3 3.4 %copy.24 = f32[5,32,64,3]{2,1,3,0:T(8,128)S(1)} copy(f32[5,32,64,3]{3,2,1,0:T(8,128)} %get-tuple-element.254) | data formatting | bytes 245760
  33.1 40.9 %all-to-all-done = f32[5,32,64,128]{3,1,0,2:T(8,128)} async-done(((f32[5,32,64,128]{3,1,0,2:T(8,128)}), f32[5,32,64,128]{3,1,0,2:T(8,128)}, u32[]{:S(2)}, u32[]{:S(2)}) %all-to-all-start) | async-done | bytes 5242912 | tf_op jit(solution)/shard_map/all_to_all | solution.py:131
  74.0 3.3 %copy.10 = f32[5,2,32,32,128]{4,2,1,3,0:T(8,128)S(1)} copy(f32[5,2,32,32,128]{4,2,0,3,1:T(8,128)} %bitcast.6) | data formatting | bytes 10485760 | tf_op jit(solution)/shard_map/all_to_all | solution.py:131
  77.3 4.2 %fusion.137 = (f32[5,62,32,128]{3,1,2,0:T(8,128)S(1)}, f32[5,62,32,128]{3,1,2,0:T(8,128)}) fusion(f32[5,64,32,128]{3,1,2,0:T(8,128)S(1)} %bitcast.63), kind=kLoop, calls=%fused_computation.147 | loop fusion | bytes 20316160 | tf_op jit(solution)/shard_map/jit(_roll_static)/slice | solution.py:59
  81.5 5.5 %fusion.139 = (f32[5,63,32,128]{3,1,2,0:T(8,128)}, f32[5,63,32,128]{3,1,2,0:T(8,128)}) fusion(f32[5,64,32,128]{3,1,2,0:T(8,128)S(1)} %bitcast.64), kind=kLoop, calls=%fused_computation.149 | loop fusion | bytes 20643840 | tf_op jit(solution)/shard_map/jit(_roll_static)/slice | solution.py:59
  87.2 10.9 %fusion.54 = f32[5,64,32,128]{3,1,2,0:T(8,128)S(1)} fusion(f32[5,1,32,128]{3,1,2,0:T(1,128)S(1)} %get-tuple-element.260, f32[5,63,32,128]{3,1,2,0:T(8,128)} %get-tuple-element.262, f32[5,63,32,128]{3,1,2,0:T(8,128)} %get-tuple-element.261, f32[5,1,32,128]{3,1,2,0:T(1,128)S(1)} %get-tuple-element.259, f32[5,2,32,128]{3,1,2,0:T(2,128)S(1)} %get-tuple-element.256, ...), kind=kOutput, calls=%fused_computation.64 | convolution fusion | flops 1018552320 | bytes 26214400 | tf_op jit(solution)/shard_map/ij,fjyz->fiyz/dot_general | solution.py:134
  98.2 5.4 %copy.11 = f32[5,64,32,128]{3,2,0,1:T(8,128)} copy(f32[5,64,32,128]{3,1,2,0:T(8,128)S(1)} %fusion.54) | data formatting | bytes 10485760 | tf_op jit(solution)/shard_map/ij,fjyz->fiyz/transpose | solution.py:134
  103.6 6.1 %all-to-all-start.1 = ((f32[5,64,32,128]{3,2,0,1:T(8,128)}), f32[5,64,32,128]{3,2,0,1:T(8,128)}, u32[]{:S(2)}, u32[]{:S(2)}) async-start(f32[5,64,32,128]{3,2,0,1:T(8,128)} %copy.11), calls=%async_computation.1 | async-start | bytes 10485760 | tf_op jit(solution)/shard_map/all_to_all | solution.py:135
  109.7 18.1 %while.43 = (s32[]{:T(128)}, f32[5]{0:T(128)S(1)}, f32[256,5]{1,0:T(8,128)S(1)}, f32[5]{0:T(128)S(1)}, f32[5]{0:T(128)S(1)}, /*index=5*/s32[]{:T(128)}, s32[]{:T(128)}) while((s32[]{:T(128)}, f32[5]{0:T(128)S(1)}, f32[256,5]{1,0:T(8,128)S(1)}, f32[5]{0:T(128)S(1)}, f32[5]{0:T(128)S(1)}, /*index=5*/s32[]{:T(128)}, s32[]{:T(128)}) %tuple.80), condition=%wide.region_1.2_spmd.clone, body=%wide.region_0.1_spmd.clone.sunk | while | flops 23 | bytes 211 | solution.py:91
  131.7 12.4 %all-reduce = f32[20]{0:T(128)S(1)} all-reduce(f32[20]{0:T(128)S(1)} %dynamic-update-slice), channel_id=2, replica_groups=mesh['gx'=2,'gy'=4,'gz'=4] {'gy'}, use_global_device_ids=true, to_apply=%add | all-reduce | flops 20 | bytes 160
  144.2 3.3 %copy.14 = f32[5,32,64,3]{3,2,1,0:T(8,128)} copy(f32[5,32,64,3]{2,1,3,0:T(8,128)S(1)} %collective-permute-done) | data formatting | bytes 245760 | tf_op jit(solution)/shard_map/ppermute | solution.py:22
  147.5 3.2 %copy.16 = f32[5,32,64,3]{3,2,1,0:T(8,128)} copy(f32[5,32,64,3]{2,1,3,0:T(8,128)S(1)} %collective-permute-done.1) | data formatting | bytes 245760 | tf_op jit(solution)/shard_map/ppermute | solution.py:21
  150.7 17.4 %all-to-all-done.1 = f32[5,64,32,128]{3,2,0,1:T(8,128)} async-done(((f32[5,64,32,128]{3,2,0,1:T(8,128)}), f32[5,64,32,128]{3,2,0,1:T(8,128)}, u32[]{:S(2)}, u32[]{:S(2)}) %all-to-all-start.1) | async-done | bytes 5242912 | tf_op jit(solution)/shard_map/all_to_all | solution.py:135
  168.0 3.3 %copy.12 = f32[5,32,2,32,128]{4,3,2,1,0:T(8,128)S(1)} copy(f32[5,32,2,32,128]{4,3,0,1,2:T(8,128)} %bitcast.12) | data formatting | bytes 10485760 | tf_op jit(solution)/shard_map/all_to_all | solution.py:135
  171.8 3.7 %fusion.40 = f32[5,32,64,128]{3,2,1,0:T(8,128)} fusion(f32[5,32,64,128]{3,2,1,0:T(8,128)S(1)} %bitcast.68, f32[5,32,2,32,128]{4,3,2,1,0:T(8,128)S(1)} %copy.12, f32[32,64,128]{2,1,0:T(8,128)S(1)} %get-tuple-element.252), kind=kLoop, calls=%fused_computation.51 | loop fusion | flops 2621440 | bytes 16777216 | tf_op jit(solution)/shard_map/sub | solution.py:136
  175.5 31.9 %fusion.57 = f32[5,32,64,128]{3,2,1,0:T(8,128)} fusion(f32[5,32,64,128]{3,2,1,0:T(8,128)} %fusion.40, f32[5,32,64,3]{3,2,1,0:T(8,128)} %copy.16, f32[5,32,64,128]{3,2,1,0:T(8,128)} %param.8, f32[5,32,64,3]{3,2,1,0:T(8,128)} %copy.14, f32[32,64,128]{2,1,0:T(8,128)S(1)} %get-tuple-element.251, f32[5,64]{1,0:T(8,128)S(1)} %reduce_window_sum.11, ...), kind=kOutput, calls=%fused_computation.65 | convolution fusion | flops 1026375680 | bytes 17043456 | tf_op jit(solution)/shard_map/fik,fxkz->fxiz/dot_general | solution.py:104
  208.6 14.7 %all-gather.1 = f32[20,32,1,128]{3,1,2,0:T(8,128)S(1)} all-gather(f32[5,32,1,128]{3,1,2,0:T(8,128)S(1)} %bitcast.71), channel_id=3, replica_groups=mesh['gx'=2,'gy'=4,'gz'=4] {'gy'}, dimensions={0}, use_global_device_ids=true | all-gather | bytes 409600 | tf_op jit(solution)/shard_map/all_gather | solution.py:31
  223.6 7.6 %fusion.51 = f32[5,32,64,128]{3,2,1,0:T(8,128)S(1)} fusion(f32[5,32,64,128]{3,2,1,0:T(8,128)} %fusion.57, f32[5,32,128]{2,1,0:T(8,128)S(1)} %get-tuple-element.195, f32[5,64]{1,0:T(8,128)S(1)} %get-tuple-element.263, f32[5,64]{1,0:T(8,128)S(1)} %get-tuple-element.248, pred[64,64]{1,0:T(8,128)(4,1)S(1)} %iota_compare_fusion), kind=kOutput, calls=%fused_computation.63 | convolution fusion | flops 1009315840 | bytes 10574336 | tf_op jit(solution)/shard_map/fik,fxkz->fxiz/dot_general | solution.py:117
  233.7 14.8 %all-gather.2 = f32[20,32,1,128]{3,1,2,0:T(8,128)S(1)} all-gather(f32[5,32,1,128]{3,1,2,0:T(8,128)S(1)} %bitcast.72), channel_id=4, replica_groups=mesh['gx'=2,'gy'=4,'gz'=4] {'gy'}, dimensions={0}, use_global_device_ids=true | all-gather | bytes 409600 | tf_op jit(solution)/shard_map/all_gather | solution.py:31
  248.8 6.2 %multiply_add_fusion = f32[5,32,64,128]{3,2,1,0:T(8,128)} fusion(f32[5,32,64,128]{3,2,1,0:T(8,128)} %copy-done, f32[5,32,128]{2,1,0:T(8,128)S(1)} %get-tuple-element.196, f32[5,64]{1,0:T(8,128)S(1)} %get-tuple-element.247), kind=kLoop, calls=%fused_computation.52 | loop fusion | flops 2621440 | bytes 10568960 | tf_op jit(solution)/shard_map/add | solution.py:126
  (556 shorter events, 24.8 us)
Async XLA Ops:
  7.9 66.1 %all-to-all-start = ((f32[5,32,64,128]{3,1,0,2:T(8,128)}), f32[5,32,64,128]{3,1,0,2:T(8,128)}, u32[]{:S(2)}, u32[]{:S(2)}) async-start(f32[5,32,64,128]{3,1,0,2:T(8,128)} %copy.9), calls=%async_computation | async-start | bytes 10485760 | tf_op jit(solution)/shard_map/all_to_all | solution.py:131
  23.4 9.6 %copy-start.1 = (f32[5]{0:T(128)S(1)}, f32[5]{0:T(128)}, u32[]{:S(2)}) copy-start(f32[5]{0:T(128)} %param.9) | copy-start | bytes 64
  26.9 117.3 %collective-permute-start = (f32[5,32,64,3]{2,1,3,0:T(8,128)S(1)}, f32[5,32,64,3]{2,1,3,0:T(8,128)S(1)}, u32[]{:S(2)}, u32[]{:S(2)}) collective-permute-start(f32[5,32,64,3]{2,1,3,0:T(8,128)S(1)} %copy.23), channel_id=1, source_target_pairs={{1,0},{2,1},{3,2},{0,3},{5,4},{6,5},{7,6},{4,7},{9,8},{10,9},{11,1... | collective-permute-start | bytes 368648 | tf_op jit(solution)/shard_map/ppermute | solution.py:22
  32.8 114.7 %collective-permute-start.1 = (f32[5,32,64,3]{2,1,3,0:T(8,128)S(1)}, f32[5,32,64,3]{2,1,3,0:T(8,128)S(1)}, u32[]{:S(2)}, u32[]{:S(2)}) collective-permute-start(f32[5,32,64,3]{2,1,3,0:T(8,128)S(1)} %copy.24), channel_id=1, source_target_pairs={{0,1},{1,2},{2,3},{3,0},{4,5},{5,6},{6,7},{7,4},{8,9},{9,10},{10,1... | collective-permute-start | bytes 368648 | tf_op jit(solution)/shard_map/ppermute | solution.py:21
  103.6 26.6 %copy-start.2 = (u32[32]{0:T(128)S(1)}, u32[32]{0:T(128)}, u32[]{:S(2)}) copy-start(u32[32]{0:T(128)} %constant.140) | copy-start | bytes 388
  103.6 64.5 %all-to-all-start.1 = ((f32[5,64,32,128]{3,2,0,1:T(8,128)}), f32[5,64,32,128]{3,2,0,1:T(8,128)}, u32[]{:S(2)}, u32[]{:S(2)}) async-start(f32[5,64,32,128]{3,2,0,1:T(8,128)} %copy.11), calls=%async_computation.1 | async-start | bytes 10485760 | tf_op jit(solution)/shard_map/all_to_all | solution.py:135
  147.5 23.9 %slice-start = ((s8[5242880]{0:T(1024)(128)(4,1)}), s8[1048576]{0:T(1024)(128)(4,1)S(1)}, s32[]{:S(2)}) async-start(s8[5242880]{0:T(1024)(128)(4,1)} %bitcast.67), calls=%async_computation.2 | async-start | bytes 2097152
  168.0 3.7 %slice-start.1 = ((s8[5242880]{0:T(1024)(128)(4,1)}), s8[4194304]{0:T(1024)(128)(4,1)S(1)}, s32[]{:S(2)}) async-start(s8[5242880]{0:T(1024)(128)(4,1)} %bitcast.67), calls=%async_computation.3 | async-start | bytes 8388608
  231.2 2.4 copy-start
where the time goes:
time: 256 us; the launch traced here: 255 us
  local copies, waits for them, and re-layouts  67.7 us (26%)
  waiting for transfers between devices  58.3 us (23%)
  matrix products  50.4 us (20%)
  blocking collectives  41.9 us (16%)
  other arithmetic  16.1 us (6%)
  starting transfers between devices  14.7 us (6%)
  loops' own time  4.97 us (2%)
    all_to_all x1, waiting for transfers between devices, shards(): lax.all_to_all(fields, 'gx', split_axis=2, concat_axis=1, tiled=True)  40.9 us
    dot_general x1, matrix products, wall_carries(): jnp.einsum('fik,fxkz->fxiz', forward_table, explicit, precision=highest)  31.9 us
    all_gather x2, blocking collectives, carried_in(): gathered = jax.tree.map(lambda a: lax.all_gather(a, axis), part)  29.5 us
    unnamed x16, local copies, waits for them, and re-layouts  18.4 us
    all_to_all x1, waiting for transfers between devices, shards(): lax.all_to_all(derivative, 'gx', split_axis=1, concat_axis=2, tiled=True)  17.4 us
    unnamed x1, blocking collectives  12.4 us
    dot_general x1, matrix products, shards(): derivative = jnp.einsum('ij,fjyz->fiyz', kernel, source, precision=highest)  10.9 us
    slice x4, local copies, waits for them, and re-layouts, shifted(): return jnp.roll(line_block, -offset, axis=1)  9.93 us
  transfers between devices with their start and end apart: 4, of which 2 were waited for; matrix products, arithmetic and copies ran while one was open for 27% of the time, Pallas kernels for 0%

commit v1 on v0

v1 whole, which is shorter than its diff:
```python
import functools
import math

import jax
import jax.numpy as jnp
from jax import lax
from jax.experimental import pallas as pl
from jax.experimental.pallas import tpu as pltpu
from jax.sharding import PartitionSpec as P

advect = 0.3
ratio = (-1.0 + math.sqrt(5.0) / 3.0) * 1.5
line_scale = -25.0 / 12.0
near_scale = 1.0 / 12.0
MESH = pl.DeviceIdType.MESH
f32 = jnp.float32
bf16 = jnp.bfloat16
GROUP = 4


def power(theta, count):
    return jnp.exp(-theta * count)


def rest(theta, count):
    return 1.0 - jnp.exp(-2.0 * theta * count)


def wall_tables(nu, place, rows, total, gm, tables, decay, f):
    shape = (rows + 16, 3 * rows)

    def theta_of(shape):
        half = 0.5 * lax.rsqrt(jnp.full(shape, nu, f32))
        return 2.0 * jnp.log(half + jnp.sqrt(1.0 + half * half))

    def scale_of(shape):
        theta = theta_of(shape)
        return power(theta, 1.0) / (nu * rest(theta, 1.0) * rest(theta, total + 1.0))

    theta = theta_of(shape)
    row = lax.broadcasted_iota(jnp.int32, shape, 0)
    lane = lax.broadcasted_iota(jnp.int32, shape, 1)
    col = jnp.bitwise_and(lane, rows - 1)
    start = place * rows
    low = (jnp.minimum(row, col) + start).astype(f32)
    high = (jnp.maximum(row, col) + start).astype(f32)
    own = (col + start).astype(f32)
    inner = scale_of(shape) * power(theta, high - low) * rest(theta, low + 1.0) * rest(theta, total - high)
    up = power(theta, (rows - col).astype(f32)) * rest(theta, own + 1.0)
    down = power(theta, (col + 1).astype(f32)) * rest(theta, total - own)
    full = jnp.where(row < rows, inner, jnp.where(row == rows, up, jnp.where(row == rows + 1, down, 0.0)))
    top = full.astype(bf16).astype(f32)
    gm[f] = jnp.where(lane >= 2 * rows, full - top, top).astype(bf16)

    shape = (rows, 128)
    theta = theta_of(shape)
    scale = scale_of(shape)
    row = lax.broadcasted_iota(jnp.int32, shape, 0)
    here = (row + start).astype(f32)
    tables[f, 0] = scale * power(theta, row.astype(f32)) * rest(theta, total - here)
    tables[f, 1] = scale * power(theta, (rows - 1 - row).astype(f32)) * rest(theta, here + 1.0)
    decay[f] = power(theta_of((8, 128)), float(rows))


def main_kernel(
    sizes, fields, viscous, v_out, t_out, c_out,
    q, e, xs, xr, zs, zr, ws, wr, gm, tables, decay, carry, merged,
    in_sem, out_sem, x_send, x_recv, z_send, z_recv, w_send, w_recv,
):
    px, py, pz = sizes
    nf, nx, ny, nz = q.shape
    blocks = nx // 32
    ix, iy, iz = lax.axis_index("gx"), lax.axis_index("gy"), lax.axis_index("gz")

    def x_at(k):
        return lax.rem(ix + k, px)

    z_up, z_down = lax.rem(iz + 1, pz), lax.rem(iz + pz - 1, pz)

    def load(f):
        return pltpu.make_async_copy(fields.at[f], q.at[f], in_sem.at[f])

    for f in range(nf):
        load(f).start()

    wr[...] = jnp.zeros_like(wr)
    barrier = pltpu.get_barrier_semaphore()
    for k in range(1, px):
        pl.semaphore_signal(barrier, inc=1, device_id={"gx": x_at(k)}, device_id_type=MESH)
    for to in (z_up, z_down):
        pl.semaphore_signal(barrier, inc=1, device_id={"gz": to}, device_id_type=MESH)
    for k in range(1, py):
        pl.semaphore_signal(barrier, inc=1, device_id={"gy": lax.rem(iy + k, py)}, device_id_type=MESH)

    def x_copy(f, k):
        return pltpu.make_async_remote_copy(
            src_ref=xs.at[f], dst_ref=xr.at[k - 1, f], send_sem=x_send.at[k - 1, f], recv_sem=x_recv.at[k - 1, f],
            device_id={"gx": x_at(k)}, device_id_type=MESH)

    def z_copy(f, side):
        return pltpu.make_async_remote_copy(
            src_ref=zs.at[side, f], dst_ref=zr.at[side, f], send_sem=z_send.at[side, f], recv_sem=z_recv.at[side, f],
            device_id={"gz": z_up if side == 0 else z_down}, device_id_type=MESH)

    def w_copy(f, side, k):
        to = lax.rem(iy + (k if side == 0 else py - k), py)
        return pltpu.make_async_remote_copy(
            src_ref=ws.at[side, f], dst_ref=wr.at[side, k - 1, f], send_sem=w_send.at[side, k - 1, f],
            recv_sem=w_recv.at[side, k - 1, f], device_id={"gy": to}, device_id_type=MESH)

    lane = lax.broadcasted_iota(jnp.int32, (ny, nz), 1)
    group = lax.shift_right_logical(lane, 2)
    zero = jnp.zeros((ny, nz), f32)

    def first_part(f, _):
        load(f).wait()

        def sums(t, state):
            fo, bo = state
            fo = ratio * (q[f, t] + fo)
            back = nx - 1 - t
            e[f, back] = bo
            bo = ratio * (q[f, back] + bo)
            return fo, bo

        fo, bo = lax.fori_loop(0, nx, sums, (zero, zero), unroll=2)
        xs[f, 0] = fo
        xs[f, 1] = q[f, nx - 1]
        xs[f, 2] = bo
        xs[f, 3] = q[f, 0]

        @pl.when(f == 0)
        def _():
            pl.semaphore_wait(barrier, px - 1 + 2 + py - 1)

        for k in range(1, px):
            x_copy(f, k).start()

        for g in range(blocks):
            def pack(t, state):
                last, lead = state
                turned = pltpu.roll(q[f, g * 32 + t], GROUP * t, 1)
                lead = jnp.where(group == t, turned, lead)
                last = jnp.where(group == jnp.bitwise_and(t + 31, 31), turned, last)
                return last, lead

            last, lead = lax.fori_loop(0, 32, pack, (zero, zero), unroll=2)
            zs[0, f, g] = last
            zs[1, f, g] = lead
        for side in range(2):
            z_copy(f, side).start()
        return 0

    lax.fori_loop(0, nf, first_part, 0)

    def build(f, _):
        wall_tables(viscous[f], iy, ny, ny * py, gm, tables, decay, f)
        return 0

    lax.fori_loop(0, nf, build, 0)
    t_copy = pltpu.make_async_copy(tables, t_out, out_sem.at[nf])
    t_copy.start()

    def second_part(f, _):
        def one(x, before):
            here = q[f, x]
            forward, previous = before
            after = jnp.where(x == nx - 1, 0.0, 1.0) * q[f, jnp.minimum(x + 1, nx - 1)]
            slope = line_scale * (e[f, x] - forward) + near_scale * (after - previous)

            def shifted(k):
                return pltpu.roll(here, (nz - k) % nz, 1)

            span = (
                0.75 * (shifted(1) - shifted(-1))
                - 0.15 * (shifted(2) - shifted(-2))
                + (1.0 / 60.0) * (shifted(3) - shifted(-3))
            )
            e[f, x] = here - advect * (q[0, x] * slope + q[2, x] * span)
            return ratio * (here + forward), here

        lax.fori_loop(0, nx, one, (zero, zero))
        return 0

    lax.fori_loop(0, nf, second_part, 0)

    inside = jnp.bitwise_and(lane, 3)
    even = jnp.bitwise_and(group, 1) == 0
    edges = jnp.logical_or(group == 0, group == nz // GROUP - 1)
    closing = 1.0 / (1.0 - ratio ** (nx * px))

    def third_part(f, _):
        for side in range(2):
            z_copy(f, side).wait_recv()
        for g in range(blocks):
            left = (zr[0, f, g] - zs[0, f, g]) * (1.0 / 60.0)
            right = (zr[1, f, g] - zs[1, f, g]) * (1.0 / 60.0)
            low = (
                jnp.where(inside == 0, -45.0 * pltpu.roll(left, nz - 3, 1), 0.0)
                + jnp.where(inside <= 1, 9.0 * pltpu.roll(left, nz - 2, 1), 0.0)
                - jnp.where(inside <= 2, pltpu.roll(left, nz - 1, 1), 0.0)
            )
            high = (
                jnp.where(inside == 3, 45.0 * pltpu.roll(right, 3, 1), 0.0)
                - jnp.where(inside >= 2, 9.0 * pltpu.roll(right, 2, 1), 0.0)
                + jnp.where(inside >= 1, pltpu.roll(right, 1, 1), 0.0)
            )
            low = pltpu.roll(low, GROUP, 1)
            high = pltpu.roll(high, nz - GROUP, 1)
            merged[g, 0] = jnp.where(even, low, high)
            merged[g, 1] = jnp.where(even, high, low)

        for k in range(1, px):
            x_copy(f, k).wait_recv()
        ahead = ratio ** (nx * (px - 1)) * xs[f, 0]
        behind = ratio ** (nx * (px - 1)) * xs[f, 2]
        for k in range(1, px):
            ahead = ahead + ratio ** (nx * (k - 1)) * xr[k - 1, f, 0]
            behind = behind + ratio ** (nx * (k - 1)) * xr[px - k - 1, f, 2]
        carry[0] = (advect * line_scale * closing) * ahead
        carry[1] = (-advect * line_scale * closing) * behind
        e[f, 0] = e[f, 0] + (advect * near_scale) * q[0, 0] * xr[0, f, 1]
        e[f, nx - 1] = e[f, nx - 1] - (advect * near_scale) * q[0, nx - 1] * xr[px - 2, f, 3]
        matrix = gm[f]

        for g in range(blocks):
            def pair(t, weights):
                fw, bw = weights
                tops, lows = [], []
                for o in range(2):
                    x = g * 32 + 2 * t + o
                    turned = pltpu.roll(merged[g, o], jnp.bitwise_and(nz - GROUP * (2 * t + o), nz - 1), 1)
                    span = jnp.where(edges, turned, 0.0)
                    whole = e[f, x] + q[0, x] * (fw * carry[0] + bw * carry[1]) - advect * q[2, x] * span
                    top = whole.astype(bf16)
                    tops.append(top)
                    lows.append((whole - top.astype(f32)).astype(bf16))
                    fw = fw * ratio
                    bw = bw * (1.0 / ratio)
                top = jnp.concatenate(tops, axis=1)
                right = jnp.concatenate([top, jnp.concatenate(lows, axis=1), top], axis=0)
                solved = jnp.dot(matrix, right, preferred_element_type=f32)
                for o in range(2):
                    x = g * 32 + 2 * t + o
                    e[f, x] = solved[:ny, o * nz : (o + 1) * nz]
                    ws[0, f, pl.ds(x, 1), :] = solved[ny : ny + 1, o * nz : (o + 1) * nz]
                    ws[1, f, pl.ds(x, 1), :] = solved[ny + 1 : ny + 2, o * nz : (o + 1) * nz]
                return fw, bw

            first = (f32(ratio ** (32 * g)), f32(ratio ** (nx - 1 - 32 * g)))
            lax.fori_loop(0, 16, pair, first)

        for k in range(1, py):
            @pl.when(iy + k < py)
            def _():
                w_copy(f, 0, k).start()

            @pl.when(iy >= k)
            def _():
                w_copy(f, 1, k).start()
        pltpu.make_async_copy(e.at[f], v_out.at[f], out_sem.at[f]).start()
        return 0

    lax.fori_loop(0, nf, third_part, 0)

    def fourth_part(f, _):
        for k in range(1, py):
            @pl.when(iy >= k)
            def _():
                w_copy(f, 0, k).wait_recv()

            @pl.when(iy + k < py)
            def _():
                w_copy(f, 1, k).wait_recv()
        step = jnp.broadcast_to(decay[f][0:1, :], (nx, nz))
        for side in range(2):
            total = wr[side, py - 2, f]
            for k in range(py - 2, 0, -1):
                total = wr[side, k - 1, f] + step * total
            c_out[side, f] = total
        return 0

    lax.fori_loop(0, nf, fourth_part, 0)

    def finish(f, _):
        for k in range(1, px):
            x_copy(f, k).wait_send()
        for side in range(2):
            z_copy(f, side).wait_send()
        for k in range(1, py):
            @pl.when(iy + k < py)
            def _():
                w_copy(f, 0, k).wait_send()

            @pl.when(iy >= k)
            def _():
                w_copy(f, 1, k).wait_send()
        pltpu.make_async_copy(e.at[f], v_out.at[f], out_sem.at[f]).wait()
        return 0

    lax.fori_loop(0, nf, finish, 0)
    t_copy.wait()


def last_kernel(v, tables, rows, out):
    for o in range(v.shape[1]):
        out[0, o] = (
            v[0, o]
            + tables[0, 0] * rows[0, 0, o : o + 1, :]
            + tables[0, 1] * rows[1, 0, o : o + 1, :]
        )


def shards(fields, viscous):
    nf, nx, ny, nz = fields.shape
    px, py, pz = (lax.axis_size(a) for a in ("gx", "gy", "gz"))
    blocks = nx // 32
    any_space = pl.BlockSpec(memory_space=pl.ANY)
    v, tables, rows = pl.pallas_call(
        functools.partial(main_kernel, (px, py, pz)),
        out_shape=(
            jax.ShapeDtypeStruct((nf, nx, ny, nz), f32),
            jax.ShapeDtypeStruct((nf, 2, ny, nz), f32),
            jax.ShapeDtypeStruct((2, nf, nx, nz), f32),
        ),
        in_specs=[any_space, pl.BlockSpec(memory_space=pltpu.SMEM)],
        out_specs=(any_space, any_space, pl.BlockSpec(memory_space=pltpu.VMEM)),
        scratch_shapes=[
            pltpu.VMEM((nf, nx, ny, nz), f32),
            pltpu.VMEM((nf, nx, ny, nz), f32),
            pltpu.VMEM((nf, 4, ny, nz), f32),
            pltpu.VMEM((px - 1, nf, 4, ny, nz), f32),
            pltpu.VMEM((2, nf, blocks, ny, nz), f32),
            pltpu.VMEM((2, nf, blocks, ny, nz), f32),
            pltpu.VMEM((2, nf, nx, nz), f32),
            pltpu.VMEM((2, py - 1, nf, nx, nz), f32),
            pltpu.VMEM((nf, ny + 16, 3 * ny), bf16),
            pltpu.VMEM((nf, 2, ny, nz), f32),
            pltpu.VMEM((nf, 8, nz), f32),
            pltpu.VMEM((2, ny, nz), f32),
            pltpu.VMEM((blocks, 2, ny, nz), f32),
            pltpu.SemaphoreType.DMA((nf,)),
            pltpu.SemaphoreType.DMA((nf + 1,)),
            pltpu.SemaphoreType.DMA((px - 1, nf)),
            pltpu.SemaphoreType.DMA((px - 1, nf)),
            pltpu.SemaphoreType.DMA((2, nf)),
            pltpu.SemaphoreType.DMA((2, nf)),
            pltpu.SemaphoreType.DMA((2, py - 1, nf)),
            pltpu.SemaphoreType.DMA((2, py - 1, nf)),
        ],
        compiler_params=pltpu.CompilerParams(
            collective_id=0, has_side_effects=True, vmem_limit_bytes=50 * 1024 * 1024
        ),
        name="section",
    )(fields, viscous)
    chunk = 16
    return pl.pallas_call(
        last_kernel,
        grid=(nf, nx // chunk),
        out_shape=jax.ShapeDtypeStruct((nf, nx, ny, nz), f32),
        in_specs=[
            pl.BlockSpec((1, chunk, ny, nz), lambda f, x: (f, x, 0, 0)),
            pl.BlockSpec((1, 2, ny, nz), lambda f, x: (f, 0, 0, 0)),
            pl.BlockSpec((2, 1, chunk, nz), lambda f, x: (0, f, x, 0)),
        ],
        out_specs=pl.BlockSpec((1, chunk, ny, nz), lambda f, x: (f, x, 0, 0)),
        compiler_params=pltpu.CompilerParams(vmem_limit_bytes=16 * 1024 * 1024),
        name="carried",
    )(v, tables, rows)


def solution(mesh):
    in_specs = (P(None, "gx", "gy", "gz"), P())
    out_specs = P(None, "gx", "gy", "gz")
    return jax.shard_map(shards, mesh=mesh, in_specs=in_specs, out_specs=out_specs, check_vma=False)
```

time: 256 us -> 66.1 us (0.26)
  local copies, waits for them, and re-layouts: 67.7 us -> 3.13 us
  Pallas kernels: 0 us -> 62.8 us
  waiting for transfers between devices: 58.3 us -> 0 us
  matrix products: 50.4 us -> 0 us
  blocking collectives: 41.9 us -> 0 us
  other arithmetic: 16.1 us -> 0 us
  starting transfers between devices: 14.7 us -> 0 us
  loops' own time: 4.97 us -> 0 us
    pallas_call x0 -> x2, Pallas kernels: none -> 62.8 us  [the longest x1 58.3 us: shards(): pl.pallas_call(functools.partial(main_kernel, (px, py, pz)), out_shape=(j...]
    all_to_all x2 -> x0, waiting for transfers between devices: 58.3 us -> none  [the longest x1 40.9 us: shards(): lax.all_to_all(fields, 'gx', split_axis=2, concat_axis=1, tiled=True)]
    dot_general x3 -> x0, matrix products: 50.4 us -> none  [the longest x1 31.9 us: wall_carries(): jnp.einsum('fik,fxkz->fxiz', forward_table, explicit, precision=highest)]
    all_gather x2 -> x0, blocking collectives: 29.5 us -> none  [carried_in(): gathered = jax.tree.map(lambda a: lax.all_gather(a, axis), part)]
    slice x8 -> x0, local copies, waits for them, and re-layouts: 20.9 us -> none  [the longest x4 9.93 us: shifted(): return jnp.roll(line_block, -offset, axis=1)]
    unnamed x16 -> x4, local copies, waits for them, and re-layouts: 18.4 us -> 3.13 us
    unnamed x1 -> x0, blocking collectives: 12.4 us -> none
    all_to_all x2 -> x0, starting transfers between devices: 12 us -> none  [the longest x1 6.08 us: shards(): lax.all_to_all(derivative, 'gx', split_axis=1, concat_axis=2, tiled=True)]
  transfers between devices with their start and end apart: 4 -> 0, of which waited for: 2 -> 0; matrix products, arithmetic and copies ran while one was open for 27% -> 0% of each run, Pallas kernels for 0% -> 0%
where the time goes in v1:
time: 66.1 us; the launch traced here: 66 us
  Pallas kernels  62.8 us (95%)
  local copies, waits for them, and re-layouts  3.13 us (5%)
    pallas_call x1, Pallas kernels, shards(): pl.pallas_call(functools.partial(main_kernel, (px, py, pz)), out_shape=(j...  58.3 us
    pallas_call x1, Pallas kernels, shards(): pl.pallas_call(last_kernel, grid=(nf, nx // chunk), out_shape=jax.ShapeDt...  4.52 us
    unnamed x4, local copies, waits for them, and re-layouts  3.13 us

profile of v1, /device:TPU:0, one launch (start us, length us, event | category | flops | bytes accessed | tf_op | source)
XLA Modules:
  0.0 66.0 jit_solution(9185112089484370593)
XLA Ops:
  0.0 0.0 copy-start.1
  0.0 0.7 copy-done.1
  0.7 58.3 %section.1 = (f32[5,32,64,128]{3,2,1,0:T(8,128)}, f32[5,2,64,128]{3,2,1,0:T(8,128)S(1)}, f32[2,5,32,128]{3,2,1,0:T(8,128)S(1)}) custom-call(f32[5,32,64,128]{3,2,1,0:T(8,128)} %fields.1, f32[5]{0:T(128)S(1)} %copy-done.1), custom_call_target="tpu_custom_call" | custom-call | tf_op jit(solution)/shard_map/section/pallas_call | solution.py:319
  58.9 0.0 copy-start
  59.0 2.5 %copy-done = f32[5,32,64,128]{3,2,1,0:T(8,128)S(1)} copy-done((f32[5,32,64,128]{3,2,1,0:T(8,128)S(1)}, f32[5,32,64,128]{3,2,1,0:T(8,128)}, u32[]{:S(2)}) %copy-start) | copy-done | bytes 5242904
  61.4 4.5 %carried.1 = f32[5,32,64,128]{3,2,1,0:T(8,128)} custom-call(f32[5,32,64,128]{3,2,1,0:T(8,128)S(1)} %copy-done, f32[5,2,64,128]{3,2,1,0:T(8,128)S(1)} %get-tuple-element.9.tables, f32[2,5,32,128]{3,2,1,0:T(8,128)S(1)} %get-tuple-element.10.rows), custom_call_target="tpu_custom_call" | custom-call | tf_op jit(solution)/shard_map/carried/pallas_call | solution.py:357
Async XLA Ops:
  0.0 0.7 copy-start.1
  58.9 2.5 %copy-start = (f32[5,32,64,128]{3,2,1,0:T(8,128)S(1)}, f32[5,32,64,128]{3,2,1,0:T(8,128)}, u32[]{:S(2)}) copy-start(f32[5,32,64,128]{3,2,1,0:T(8,128)} %get-tuple-element.8.v) | copy-start | bytes 15728644

commit v2 on v1

--- a/solution.py
+++ b/solution.py
@@ -16,6 +16,9 @@
 f32 = jnp.float32
 bf16 = jnp.bfloat16
 GROUP = 4
+STEP = 8
+SPAN_STEP = 8
+PART = 8
 
 
 def power(theta, count):
@@ -63,9 +66,9 @@
 
 
 def main_kernel(
-    sizes, fields, viscous, v_out, t_out, c_out,
-    q, e, xs, xr, zs, zr, ws, wr, gm, tables, decay, carry, merged,
-    in_sem, out_sem, x_send, x_recv, z_send, z_recv, w_send, w_recv,
+    sizes, fields, viscous, e, tables, c_out,
+    q, sp, xs, xr, zs, zr, ws, wr, gm, decay, carry, merged, speeds, stencil,
+    in_sem, x_send, x_recv, z_send, z_recv, w_send, w_recv,
 ):
     px, py, pz = sizes
     nf, nx, ny, nz = q.shape
@@ -123,7 +126,7 @@
             bo = ratio * (q[f, back] + bo)
             return fo, bo
 
-        fo, bo = lax.fori_loop(0, nx, sums, (zero, zero), unroll=2)
+        fo, bo = lax.fori_loop(0, nx, sums, (zero, zero), unroll=4)
         xs[f, 0] = fo
         xs[f, 1] = q[f, nx - 1]
         xs[f, 2] = bo
@@ -136,6 +139,11 @@
         for k in range(1, px):
             x_copy(f, k).start()
 
+        return 0
+
+    lax.fori_loop(0, nf, first_part, 0)
+
+    def pack_part(f, _):
         for g in range(blocks):
             def pack(t, state):
                 last, lead = state
@@ -144,45 +152,47 @@
                 last = jnp.where(group == jnp.bitwise_and(t + 31, 31), turned, last)
                 return last, lead
 
-            last, lead = lax.fori_loop(0, 32, pack, (zero, zero), unroll=2)
+            last, lead = lax.fori_loop(0, 32, pack, (zero, zero), unroll=4)
             zs[0, f, g] = last
             zs[1, f, g] = lead
         for side in range(2):
             z_copy(f, side).start()
         return 0
 
-    lax.fori_loop(0, nf, first_part, 0)
+    lax.fori_loop(0, nf, pack_part, 0)
 
     def build(f, _):
         wall_tables(viscous[f], iy, ny, ny * py, gm, tables, decay, f)
         return 0
 
     lax.fori_loop(0, nf, build, 0)
-    t_copy = pltpu.make_async_copy(tables, t_out, out_sem.at[nf])
-    t_copy.start()
-
-    def second_part(f, _):
-        def one(x, before):
-            here = q[f, x]
-            forward, previous = before
-            after = jnp.where(x == nx - 1, 0.0, 1.0) * q[f, jnp.minimum(x + 1, nx - 1)]
-            slope = line_scale * (e[f, x] - forward) + near_scale * (after - previous)
-
-            def shifted(k):
-                return pltpu.roll(here, (nz - k) % nz, 1)
-
-            span = (
-                0.75 * (shifted(1) - shifted(-1))
-                - 0.15 * (shifted(2) - shifted(-2))
-                + (1.0 / 60.0) * (shifted(3) - shifted(-3))
-            )
-            e[f, x] = here - advect * (q[0, x] * slope + q[2, x] * span)
-            return ratio * (here + forward), here
-
-        lax.fori_loop(0, nx, one, (zero, zero))
-        return 0
-
-    lax.fori_loop(0, nf, second_part, 0)
+
+    source = jnp.bitwise_and(lax.broadcasted_iota(jnp.int32, (2 * nz, nz), 0), nz - 1)
+    target = lax.broadcasted_iota(jnp.int32, (2 * nz, nz), 1)
+    reach = jnp.bitwise_and(source - target, nz - 1)
+    weights = jnp.zeros((2 * nz, nz), f32)
+    for k, c in ((1, 45.0), (2, -9.0), (3, 1.0)):
+        weights = jnp.where(reach == k, c, jnp.where(reach == nz - k, -c, weights))
+    stencil[...] = weights.astype(bf16)
+
+    def scale_speeds(x, _):
+        speeds[0, x] = (-advect * line_scale) * q[0, x]
+        speeds[1, x] = (-advect / 60.0) * q[2, x]
+        return 0
+
+    lax.fori_loop(0, nx, scale_speeds, 0, unroll=4)
+
+    def span_part(f):
+        def some(t, _):
+            here = q[f, pl.ds(t * SPAN_STEP, SPAN_STEP)].reshape(SPAN_STEP * ny, nz)
+            top = here.astype(bf16)
+            low = (here - top.astype(f32)).astype(bf16)
+            both = jnp.concatenate([top, low], axis=1)
+            made = jnp.dot(both, stencil[...], preferred_element_type=f32)
+            sp[pl.ds(t * SPAN_STEP, SPAN_STEP)] = made.reshape(SPAN_STEP, ny, nz)
+            return 0
+
+        lax.fori_loop(0, nx // SPAN_STEP, some, 0)
 
     inside = jnp.bitwise_and(lane, 3)
     even = jnp.bitwise_and(group, 1) == 0
@@ -190,11 +200,12 @@
     closing = 1.0 / (1.0 - ratio ** (nx * px))
 
     def third_part(f, _):
+        span_part(f)
         for side in range(2):
             z_copy(f, side).wait_recv()
         for g in range(blocks):
-            left = (zr[0, f, g] - zs[0, f, g]) * (1.0 / 60.0)
-            right = (zr[1, f, g] - zs[1, f, g]) * (1.0 / 60.0)
+            left = zr[0, f, g] - zs[0, f, g]
+            right = zr[1, f, g] - zs[1, f, g]
             low = (
                 jnp.where(inside == 0, -45.0 * pltpu.roll(left, nz - 3, 1), 0.0)
                 + jnp.where(inside <= 1, 9.0 * pltpu.roll(left, nz - 2, 1), 0.0)
@@ -217,38 +228,43 @@
         for k in range(1, px):
             ahead = ahead + ratio ** (nx * (k - 1)) * xr[k - 1, f, 0]
             behind = behind + ratio ** (nx * (k - 1)) * xr[px - k - 1, f, 2]
-        carry[0] = (advect * line_scale * closing) * ahead
-        carry[1] = (-advect * line_scale * closing) * behind
-        e[f, 0] = e[f, 0] + (advect * near_scale) * q[0, 0] * xr[0, f, 1]
-        e[f, nx - 1] = e[f, nx - 1] - (advect * near_scale) * q[0, nx - 1] * xr[px - 2, f, 3]
+        carry[0] = closing * behind
         matrix = gm[f]
-
-        for g in range(blocks):
-            def pair(t, weights):
-                fw, bw = weights
-                tops, lows = [], []
-                for o in range(2):
-                    x = g * 32 + 2 * t + o
-                    turned = pltpu.roll(merged[g, o], jnp.bitwise_and(nz - GROUP * (2 * t + o), nz - 1), 1)
-                    span = jnp.where(edges, turned, 0.0)
-                    whole = e[f, x] + q[0, x] * (fw * carry[0] + bw * carry[1]) - advect * q[2, x] * span
-                    top = whole.astype(bf16)
-                    tops.append(top)
-                    lows.append((whole - top.astype(f32)).astype(bf16))
-                    fw = fw * ratio
-                    bw = bw * (1.0 / ratio)
-                top = jnp.concatenate(tops, axis=1)
-                right = jnp.concatenate([top, jnp.concatenate(lows, axis=1), top], axis=0)
-                solved = jnp.dot(matrix, right, preferred_element_type=f32)
-                for o in range(2):
-                    x = g * 32 + 2 * t + o
-                    e[f, x] = solved[:ny, o * nz : (o + 1) * nz]
-                    ws[0, f, pl.ds(x, 1), :] = solved[ny : ny + 1, o * nz : (o + 1) * nz]
-                    ws[1, f, pl.ds(x, 1), :] = solved[ny + 1 : ny + 2, o * nz : (o + 1) * nz]
-                return fw, bw
-
-            first = (f32(ratio ** (32 * g)), f32(ratio ** (nx - 1 - 32 * g)))
-            lax.fori_loop(0, 16, pair, first)
+        end = xr[px - 2, f, 3]
+
+        def some(t, state):
+            forward, previous, bw = state
+            base = t * STEP
+            block = base // 32
+            place = base - block * 32
+            tops, lows = [], []
+            for o in range(STEP):
+                x = base + o
+                here = q[f, x]
+                if o < STEP - 1:
+                    after = q[f, x + 1]
+                else:
+                    after = jnp.where(x == nx - 1, end, q[f, jnp.minimum(x + 1, nx - 1)])
+                turn = jnp.bitwise_and(nz - GROUP * (place + o), nz - 1)
+                span = sp[x] + jnp.where(edges, pltpu.roll(merged[block, o % 2], turn, 1), 0.0)
+                slope = (e[f, x] - forward) + bw * carry[0] + (near_scale / line_scale) * (after - previous)
+                whole = here + speeds[0, x] * slope + speeds[1, x] * span
+                top = whole.astype(bf16)
+                tops.append(top)
+                lows.append((whole - top.astype(f32)).astype(bf16))
+                forward = ratio * (here + forward)
+                previous = here
+                bw = bw * (1.0 / ratio)
+            top = jnp.concatenate(tops, axis=1)
+            right = jnp.concatenate([top, jnp.concatenate(lows, axis=1), top], axis=0)
+            solved = jnp.dot(matrix, right, preferred_element_type=f32)
+            for o in range(STEP):
+                e[f, base + o] = solved[:ny, o * nz : (o + 1) * nz]
+                ws[0, f, pl.ds(base + o, 1), :] = solved[ny : ny + 1, o * nz : (o + 1) * nz]
+                ws[1, f, pl.ds(base + o, 1), :] = solved[ny + 1 : ny + 2, o * nz : (o + 1) * nz]
+            return forward, previous, bw
+
+        lax.fori_loop(0, nx // STEP, some, (closing * ahead, xr[0, f, 1], f32(ratio ** (nx - 1))))
 
         for k in range(1, py):
             @pl.when(iy + k < py)
@@ -258,7 +274,6 @@
             @pl.when(iy >= k)
             def _():
                 w_copy(f, 1, k).start()
-        pltpu.make_async_copy(e.at[f], v_out.at[f], out_sem.at[f]).start()
         return 0
 
     lax.fori_loop(0, nf, third_part, 0)
@@ -295,26 +310,42 @@
             @pl.when(iy >= k)
             def _():
                 w_copy(f, 1, k).wait_send()
-        pltpu.make_async_copy(e.at[f], v_out.at[f], out_sem.at[f]).wait()
         return 0
 
     lax.fori_loop(0, nf, finish, 0)
-    t_copy.wait()
-
-
-def last_kernel(v, tables, rows, out):
-    for o in range(v.shape[1]):
-        out[0, o] = (
-            v[0, o]
-            + tables[0, 0] * rows[0, 0, o : o + 1, :]
-            + tables[0, 1] * rows[1, 0, o : o + 1, :]
-        )
+
+
+def last_kernel(v, tables, rows, out, made, sem):
+    nf, nx = v.shape[:2]
+    parts = nx // PART
+
+    def copy(t):
+        f, x = t // parts, (t % parts) * PART
+        return pltpu.make_async_copy(made.at[f, pl.ds(x, PART)], out.at[f, pl.ds(x, PART)], sem.at[t])
+
+    def some(t, _):
+        f, x = t // parts, (t % parts) * PART
+        up, down = tables[f, 0], tables[f, 1]
+        for o in range(PART):
+            made[f, x + o] = v[f, x + o] + up * rows[0, f, pl.ds(x + o, 1), :] + down * rows[1, f, pl.ds(x + o, 1), :]
+        copy(t).start()
+        return 0
+
+    lax.fori_loop(0, nf * parts, some, 0)
+
+    def finish(t, _):
+        copy(t).wait()
+        return 0
+
+    lax.fori_loop(0, nf * parts, finish, 0)
 
 
 def shards(fields, viscous):
     nf, nx, ny, nz = fields.shape
     px, py, pz = (lax.axis_size(a) for a in ("gx", "gy", "gz"))
     blocks = nx // 32
+    in_vmem = pl.BlockSpec(memory_space=pltpu.VMEM)
+    size = 4 * nf * nx * ny * nz
     any_space = pl.BlockSpec(memory_space=pl.ANY)
     v, tables, rows = pl.pallas_call(
         functools.partial(main_kernel, (px, py, pz)),
@@ -323,11 +354,11 @@
             jax.ShapeDtypeStruct((nf, 2, ny, nz), f32),
             jax.ShapeDtypeStruct((2, nf, nx, nz), f32),
         ),
-        in_specs=[any_space, pl.BlockSpec(memory_space=pltpu.SMEM)],
-        out_specs=(any_space, any_space, pl.BlockSpec(memory_space=pltpu.VMEM)),
+        in_specs=[pl.BlockSpec(memory_space=pltpu.HBM), pl.BlockSpec(memory_space=pltpu.SMEM)],
+        out_specs=(in_vmem, in_vmem, in_vmem),
         scratch_shapes=[
             pltpu.VMEM((nf, nx, ny, nz), f32),
-            pltpu.VMEM((nf, nx, ny, nz), f32),
+            pltpu.VMEM((nx, ny, nz), f32),
             pltpu.VMEM((nf, 4, ny, nz), f32),
             pltpu.VMEM((px - 1, nf, 4, ny, nz), f32),
             pltpu.VMEM((2, nf, blocks, ny, nz), f32),
@@ -335,12 +366,12 @@
             pltpu.VMEM((2, nf, nx, nz), f32),
             pltpu.VMEM((2, py - 1, nf, nx, nz), f32),
             pltpu.VMEM((nf, ny + 16, 3 * ny), bf16),
-            pltpu.VMEM((nf, 2, ny, nz), f32),
             pltpu.VMEM((nf, 8, nz), f32),
             pltpu.VMEM((2, ny, nz), f32),
             pltpu.VMEM((blocks, 2, ny, nz), f32),
+            pltpu.VMEM((2, nx, ny, nz), f32),
+            pltpu.VMEM((2 * nz, nz), bf16),
             pltpu.SemaphoreType.DMA((nf,)),
-            pltpu.SemaphoreType.DMA((nf + 1,)),
             pltpu.SemaphoreType.DMA((px - 1, nf)),
             pltpu.SemaphoreType.DMA((px - 1, nf)),
             pltpu.SemaphoreType.DMA((2, nf)),
@@ -349,22 +380,20 @@
             pltpu.SemaphoreType.DMA((2, py - 1, nf)),
         ],
         compiler_params=pltpu.CompilerParams(
-            collective_id=0, has_side_effects=True, vmem_limit_bytes=50 * 1024 * 1024
+            collective_id=0, has_side_effects=True, vmem_limit_bytes=min(5 * size, 56 << 20)
         ),
         name="section",
     )(fields, viscous)
-    chunk = 16
     return pl.pallas_call(
         last_kernel,
-        grid=(nf, nx // chunk),
         out_shape=jax.ShapeDtypeStruct((nf, nx, ny, nz), f32),
-        in_specs=[
-            pl.BlockSpec((1, chunk, ny, nz), lambda f, x: (f, x, 0, 0)),
-            pl.BlockSpec((1, 2, ny, nz), lambda f, x: (f, 0, 0, 0)),
-            pl.BlockSpec((2, 1, chunk, nz), lambda f, x: (0, f, x, 0)),
+        in_specs=[in_vmem, in_vmem, in_vmem],
+        out_specs=any_space,
+        scratch_shapes=[
+            pltpu.VMEM((nf, nx, ny, nz), f32),
+            pltpu.SemaphoreType.DMA((nf * (nx // PART),)),
         ],
-        out_specs=pl.BlockSpec((1, chunk, ny, nz), lambda f, x: (f, x, 0, 0)),
-        compiler_params=pltpu.CompilerParams(vmem_limit_bytes=16 * 1024 * 1024),
+        compiler_params=pltpu.CompilerParams(vmem_limit_bytes=min(3 * size, 48 << 20)),
         name="carried",
     )(v, tables, rows)
 

time: 66.1 us -> 35.2 us (0.53)
  Pallas kernels: 62.8 us -> 31.8 us
    pallas_call x1, Pallas kernels: 58.3 us -> 29.3 us  [shards(): pl.pallas_call(functools.partial(main_kernel, (px, py, pz)), out_shape=(j...]
    pallas_call x1, Pallas kernels: 4.52 us -> 2.54 us  [shards(): pl.pallas_call(last_kernel, out_shape=jax.ShapeDtypeStruct((nf, nx, ny, n...]
where the time goes in v2:
time: 35.2 us; the launch traced here: 35 us
  Pallas kernels  31.8 us (90%)
  local copies, waits for them, and re-layouts  3.14 us (9%)
    pallas_call x1, Pallas kernels, shards(): pl.pallas_call(functools.partial(main_kernel, (px, py, pz)), out_shape=(j...  29.3 us
    unnamed x4, local copies, waits for them, and re-layouts  3.14 us
    pallas_call x1, Pallas kernels, shards(): pl.pallas_call(last_kernel, out_shape=jax.ShapeDtypeStruct((nf, nx, ny, n...  2.54 us

profile of v2, /device:TPU:0, one launch (start us, length us, event | category | flops | bytes accessed | tf_op | source)
XLA Modules:
  0.0 35.0 jit_solution(5850248012077101982)
XLA Ops:
  0.0 0.0 copy-start
  0.0 2.5 %copy-done = f32[5,32,64,128]{3,2,1,0:T(8,128)S(1)} copy-done((f32[5,32,64,128]{3,2,1,0:T(8,128)S(1)}, f32[5,32,64,128]{3,2,1,0:T(8,128)}, u32[]{:S(2)}) %copy-start) | copy-done | bytes 5242904
  2.5 0.0 copy-start.1
  2.5 0.7 %copy-done.1 = f32[5]{0:T(128)S(1)} copy-done((f32[5]{0:T(128)S(1)}, f32[5]{0:T(128)}, u32[]{:S(2)}) %copy-start.1) | copy-done | bytes 44
  3.1 29.3 %section.1 = (f32[5,32,64,128]{3,2,1,0:T(8,128)S(1)}, f32[5,2,64,128]{3,2,1,0:T(8,128)S(1)}, f32[2,5,32,128]{3,2,1,0:T(8,128)S(1)}) custom-call(f32[5,32,64,128]{3,2,1,0:T(8,128)S(1)} %copy-done, f32[5]{0:T(128)S(1)} %copy-done.1), custom_call_target="tpu_custom_call" | custom-call | tf_op jit(solution)/shard_map/section/pallas_call | solution.py:350
  32.5 2.5 %carried.1 = f32[5,32,64,128]{3,2,1,0:T(8,128)} custom-call(f32[5,32,64,128]{3,2,1,0:T(8,128)S(1)} %get-tuple-element.8.v, f32[5,2,64,128]{3,2,1,0:T(8,128)S(1)} %get-tuple-element.9.tables, f32[2,5,32,128]{3,2,1,0:T(8,128)S(1)} %get-tuple-element.10.rows), custom_call_target="tpu_custom_call" | custom-call | tf_op jit(solution)/shard_map/carried/pallas_call | solution.py:387
Async XLA Ops:
  0.0 2.5 %copy-start = (f32[5,32,64,128]{3,2,1,0:T(8,128)S(1)}, f32[5,32,64,128]{3,2,1,0:T(8,128)}, u32[]{:S(2)}) copy-start(f32[5,32,64,128]{3,2,1,0:T(8,128)} %fields.1) | copy-start | bytes 15728644
  2.5 0.7 %copy-start.1 = (f32[5]{0:T(128)S(1)}, f32[5]{0:T(128)}, u32[]{:S(2)}) copy-start(f32[5]{0:T(128)} %viscous.1) | copy-start | bytes 64

commit v3 on v2

--- a/solution.py
+++ b/solution.py
@@ -16,8 +16,8 @@
 f32 = jnp.float32
 bf16 = jnp.bfloat16
 GROUP = 4
-STEP = 8
-SPAN_STEP = 8
+STEP = 16
+SPAN_STEP = 16
 PART = 8
 
 
@@ -126,7 +126,7 @@
             bo = ratio * (q[f, back] + bo)
             return fo, bo
 
-        fo, bo = lax.fori_loop(0, nx, sums, (zero, zero), unroll=4)
+        fo, bo = lax.fori_loop(0, nx, sums, (zero, zero), unroll=8)
         xs[f, 0] = fo
         xs[f, 1] = q[f, nx - 1]
         xs[f, 2] = bo
@@ -152,7 +152,7 @@
                 last = jnp.where(group == jnp.bitwise_and(t + 31, 31), turned, last)
                 return last, lead
 
-            last, lead = lax.fori_loop(0, 32, pack, (zero, zero), unroll=4)
+            last, lead = lax.fori_loop(0, 32, pack, (zero, zero), unroll=8)
             zs[0, f, g] = last
             zs[1, f, g] = lead
         for side in range(2):
@@ -380,7 +380,7 @@
             pltpu.SemaphoreType.DMA((2, py - 1, nf)),
         ],
         compiler_params=pltpu.CompilerParams(
-            collective_id=0, has_side_effects=True, vmem_limit_bytes=min(5 * size, 56 << 20)
+            collective_id=0, has_side_effects=True, vmem_limit_bytes=47 << 20
         ),
         name="section",
     )(fields, viscous)

time: 35.2 us -> 31.1 us (0.88)
  local copies, waits for them, and re-layouts: 3.14 us -> 0.65 us
  Pallas kernels: 31.8 us -> 30.3 us
    unnamed x4 -> x2, local copies, waits for them, and re-layouts: 3.14 us -> 0.65 us
    pallas_call x1, Pallas kernels: 29.3 us -> 27.7 us  [shards(): pl.pallas_call(functools.partial(main_kernel, (px, py, pz)), out_shape=(j...]
where the time goes in v3:
time: 31.1 us; the launch traced here: 30.9 us
  Pallas kernels  30.3 us (97%)
  local copies, waits for them, and re-layouts  0.65 us (2%)
    pallas_call x1, Pallas kernels, shards(): pl.pallas_call(functools.partial(main_kernel, (px, py, pz)), out_shape=(j...  27.7 us
    pallas_call x1, Pallas kernels, shards(): pl.pallas_call(last_kernel, out_shape=jax.ShapeDtypeStruct((nf, nx, ny, n...  2.54 us
    unnamed x2, local copies, waits for them, and re-layouts  0.65 us

profile of v3, /device:TPU:0, one launch (start us, length us, event | category | flops | bytes accessed | tf_op | source)
XLA Modules:
  0.0 30.9 jit_solution(3155611417121885587)
XLA Ops:
  0.0 0.0 copy-start
  0.0 0.7 %copy-done = f32[5]{0:T(128)S(1)} copy-done((f32[5]{0:T(128)S(1)}, f32[5]{0:T(128)}, u32[]{:S(2)}) %copy-start) | copy-done | bytes 44
  0.7 27.7 %section.1 = (f32[5,32,64,128]{3,2,1,0:T(8,128)S(1)}, f32[5,2,64,128]{3,2,1,0:T(8,128)S(1)}, f32[2,5,32,128]{3,2,1,0:T(8,128)S(1)}) custom-call(f32[5,32,64,128]{3,2,1,0:T(8,128)} %fields.1, f32[5]{0:T(128)S(1)} %copy-done), custom_call_target="tpu_custom_call" | custom-call | tf_op jit(solution)/shard_map/section/pallas_call | solution.py:350
  28.4 2.5 %carried.1 = f32[5,32,64,128]{3,2,1,0:T(8,128)} custom-call(f32[5,32,64,128]{3,2,1,0:T(8,128)S(1)} %get-tuple-element.8.v, f32[5,2,64,128]{3,2,1,0:T(8,128)S(1)} %get-tuple-element.9.tables, f32[2,5,32,128]{3,2,1,0:T(8,128)S(1)} %get-tuple-element.10.rows), custom_call_target="tpu_custom_call" | custom-call | tf_op jit(solution)/shard_map/carried/pallas_call | solution.py:387
Async XLA Ops:
  0.0 0.7 %copy-start = (f32[5]{0:T(128)S(1)}, f32[5]{0:T(128)}, u32[]{:S(2)}) copy-start(f32[5]{0:T(128)} %viscous.1) | copy-start | bytes 64
